TPU v7x, 512 devices: a whole 4x4x16 slice. The times are simulated.
512 devices in a mesh: row: 16 (over z_lo, x), col: 32 (over y, z_hi, core).
Axes of the slice: x: 4, y: 4, z: 16 (z_hi: 4, z_lo: 4; z = z_hi * 4 + z_lo), core: 2. Of those that a mesh axis runs over, the one named last changes fastest.
Arguments:
- x_cols: bfloat16 [8, 262144], P(None, ('col', 'row')), may hold values from -6 to 6
- diag_rows: float32 [262144], P(('row', 'col')), may hold values from 0.5 to 2
- theta: float32 [8], replicated, may hold values from -1 to 1
- tiles: bfloat16 [16, 32, 96, 128, 128], P('row', 'col'), may hold values from -0.109375 to 0.109375
- tile_rows: int32 [16, 32, 96], P('row', 'col'), may hold values from 0 to 127, as said below
- tile_cols: int32 [16, 32, 96], P('row', 'col'), may hold values from 0 to 63, as said below
- counts: int32 [16, 32], P('row', 'col'), may hold values from 48 to 96, as said below
Outputs:
- resid: float32 [8, 262144], P(None, ('row', 'col'))
- image: float32 [8, 262144], P(None, ('col', 'row'))
Inputs may be any that keep to these rules, and one draw needn't show every extreme that they name: Within one device block, the pairs (tile_rows, tile_cols) of its 96 slots are all different. `tile_cols`: paired with tile_rows slot by slot. `counts`: slots at or past a block's count are unused and their tiles hold arbitrary values. Some block has all 96 slots in use.
All inputs are finite; a program needn't handle non-finite values.
Results may differ from a plain program's by a relative error of at most 0.0023.
Values may be sent and summed in bfloat16 or wider, within the bound.
No kernel may reach another device: no remote copies, remote signals or barrier semaphores. Data moves between devices by JAX's collectives and lax.ppermute only.
A program may use at most 64 MiB of HBM per device.

v0:
```python
import jax
import jax.numpy as jnp
from jax import lax
from jax.sharding import PartitionSpec as P


def flatten_blocks(blocks):
    return blocks.transpose(1, 0, 2).reshape(blocks.shape[1], -1)


def body(x_cols, diag_rows, theta, tiles, tile_rows, tile_cols, counts):
    row_devices = lax.axis_size("row")
    column_devices = lax.axis_size("col")
    fold_ratio = column_devices // row_devices
    vectors = x_cols.shape[0]
    own_states = x_cols.shape[1]
    blocks_here = tiles[0, 0]
    rows_here = tile_rows[0, 0]
    cols_here = tile_cols[0, 0]
    slot_count = blocks_here.shape[0]
    tile_width = blocks_here.shape[1]
    in_use = jnp.arange(slot_count, dtype=jnp.int32) < counts[0, 0]
    block_rows = own_states * column_devices // tile_width
    block_cols = own_states * row_devices // tile_width
    share_rows = own_states // tile_width
    column_vectors = lax.all_gather(x_cols, "row", axis=1, tiled=True)
    column_tiles = column_vectors.reshape(vectors, block_cols, tile_width).transpose(1, 0, 2)
    picked = jnp.take(column_tiles, cols_here, axis=0)
    products = jnp.einsum("kab,knb->kna", blocks_here, picked, preferred_element_type=jnp.float32)
    products = jnp.where(in_use[:, None, None], products, 0.0)
    partial_value = jax.ops.segment_sum(products, rows_here, num_segments=block_rows)
    on_diag = (lax.axis_index("row") == lax.axis_index("col") // fold_ratio).astype(jnp.float32)
    offset = lax.axis_index("col") % fold_ratio * block_cols
    shift_term = -theta[None, :, None] * column_tiles.astype(jnp.float32) * on_diag
    current = lax.dynamic_slice_in_dim(partial_value, offset, block_cols, 0)
    partial_value = lax.dynamic_update_slice_in_dim(partial_value, current + shift_term, offset, 0)
    scales = lax.all_gather(diag_rows, "col", axis=0, tiled=True)
    summed = lax.psum(partial_value, "col")
    scaled = (summed / scales.reshape(-1, 1, tile_width)).astype(jnp.bfloat16)
    resid_part = lax.dynamic_slice_in_dim(summed, lax.axis_index("col") * share_rows, share_rows, 0)
    picked_rows = jnp.take(scaled, rows_here, axis=0)
    transposed = jnp.einsum(
        "kab,kna->knb", blocks_here, picked_rows, preferred_element_type=jnp.float32
    )
    transposed = jnp.where(in_use[:, None, None], transposed, 0.0)
    partial_back = jax.ops.segment_sum(transposed, cols_here, num_segments=block_cols)
    image_part = lax.psum_scatter(partial_back, "row", scatter_dimension=0, tiled=True)
    return (flatten_blocks(resid_part), flatten_blocks(image_part))


def solution(mesh):
    return jax.shard_map(
        body,
        mesh=mesh,
        in_specs=(
            P(None, ("col", "row")),
            P(("row", "col")),
            P(),
            P("row", "col", None, None, None),
            P("row", "col", None),
            P("row", "col", None),
            P("row", "col"),
        ),
        out_specs=(P(None, ("row", "col")), P(None, ("col", "row"))),
        check_vma=False,
    )
```

profile of v0, /device:TPU:8, one launch (start us, length us, event | category | flops | bytes accessed | tf_op | source)
XLA Modules:
  0.0 519.1 jit_solution(790691710098318919)
XLA Ops:
  7.2 0.0 copy-start
  7.2 0.0 copy-start.4
  7.2 0.0 all-reduce.2.cloned.1.call-start
  7.2 44.6 %all_gather.6 = bf16[8,8192]{1,0:T(8,128)(2,1)S(1)} all-gather(bf16[8,512]{1,0:T(8,128)(2,1)} %param.7), channel_id=1, replica_groups=mesh['row'=16,'col'=32] {'row'}, dimensions={1}, use_global_device_ids=true | all-gather | bytes 139264 | tf_op jit(solution)/shard_map/all_gather | solution.py:26
  51.8 0.7 fusion.16
  53.1 0.7 compare_and_fusion.1
  53.8 0.7 neg.4
  54.5 0.7 gather_fusion
  55.1 0.0 copy-done
  55.1 0.0 copy-start.3
  55.2 2.5 fusion.4
  57.7 0.8 broadcast_in_dim.43
  58.5 0.0 copy-done.4
  58.5 10.8 %scatter_fusion = f32[128,8,128]{2,1,0:T(8,128)} fusion(f32[128,8,128]{2,1,0:T(8,128)} %broadcast_in_dim.43, s32[96]{0:T(128)S(1)} %bitcast.40, f32[96,8,128]{2,1,0:T(8,128)} %fusion.4), kind=kCustom, calls=%fused_computation.2 | custom fusion | flops 98304 | bytes 1180032 | tf_op jit(solution)/shard_map/scatter-add | solution.py:31
  69.3 0.0 copy-start.2
  69.3 1.8 add_dynamic-update-slice_fusion
  71.1 0.0 all-reduce.2.cloned.1.call-update
  71.1 0.0 reduce-scatter.2.cloned.1.call-start
  71.2 0.0 copy-done.3
  71.2 52.4 %all-gather = f32[32,1,512]{2,1,0:T(1,128)S(1)} all-gather(f32[1,1,512]{2,1,0:T(1,128)S(1)} %bitcast.39), channel_id=1, replica_groups=mesh['row'=16,'col'=32] {'col'}, dimensions={0}, use_global_device_ids=true | all-gather | bytes 67584 | tf_op jit(solution)/shard_map/all_gather | solution.py:37
  123.6 278.2 %all-reduce.2.cloned.1.call-done = f32[128,8,128]{2,1,0:T(8,128)} async-done(((f32[128,8,128]{2,1,0:T(8,128)}), f32[128,8,128]{2,1,0:T(8,128)}) %all-reduce.2.cloned.1.call-update) | async-done | bytes 524304 | tf_op jit(solution)/shard_map/psum | solution.py:38
  401.8 1.1 divide_convert_fusion
  402.9 1.3 gather_fusion.1
  404.3 2.7 fusion.7
  407.0 0.0 copy-done.2
  407.0 7.3 %scatter_fusion.1 = f32[64,8,128]{2,1,0:T(8,128)S(1)} fusion(f32[64,8,128]{2,1,0:T(8,128)S(1)} %broadcast_in_dim.48, s32[96]{0:T(128)S(1)} %bitcast.38, f32[96,8,128]{2,1,0:T(8,128)} %fusion.7), kind=kCustom, calls=%fused_computation.3 | custom fusion | flops 98304 | bytes 1180032 | tf_op jit(solution)/shard_map/scatter-add | solution.py:46
  414.2 0.0 copy-start.1
  414.3 0.7 copy-done.1
  414.9 0.0 reduce-scatter.2.cloned.1.call-update
  415.0 1.3 dynamic-slice_bitcast_fusion
  416.3 96.0 %reduce-scatter.2.cloned.1.call-done = f32[4,8,128]{2,1,0:T(8,128)} async-done(((f32[64,8,128]{2,1,0:T(8,128)}), f32[4,8,128]{2,1,0:T(8,128)}) %reduce-scatter.2.cloned.1.call-update) | async-done | bytes 16400 | tf_op jit(solution)/shard_map/reduce_scatter | solution.py:47
  (5 shorter events, 0.0 us)
Async XLA Ops:
  7.2 48.0 %copy-start = (bf16[1,1,96,128,128]{4,3,2,1,0:T(8,128)(2,1)S(1)}, bf16[1,1,96,128,128]{4,3,2,1,0:T(8,128)(2,1)}, u32[]{:S(2)}) copy-start(bf16[1,1,96,128,128]{4,3,2,1,0:T(8,128)(2,1)} %param.10) | copy-start | bytes 9437188
  7.2 51.3 %copy-start.4 = (s32[1,1,96]{2,1,0:T(1,128)S(1)}, s32[1,1,96]{2,1,0:T(1,128)}, u32[]{:S(2)}) copy-start(s32[1,1,96]{2,1,0:T(1,128)} %param.11) | copy-start | bytes 1156
  7.2 394.6 %all-reduce.2.cloned.1.call-start = ((), (), s32[]{:S(2)}) async-start(), calls=%async_computation.1 | async-start | bytes 1048576 | tf_op jit(solution)/shard_map/psum | solution.py:38
  55.1 16.0 %copy-start.3 = (f32[512]{0:T(512)S(1)}, f32[512]{0:T(512)}, u32[]{:S(2)}) copy-start(f32[512]{0:T(512)} %param.8) | copy-start | bytes 6148
  69.3 337.6 %copy-start.2 = (s32[1,1,96]{2,1,0:T(1,128)S(1)}, s32[1,1,96]{2,1,0:T(1,128)}, u32[]{:S(2)}) copy-start(s32[1,1,96]{2,1,0:T(1,128)} %param.12) | copy-start | bytes 1156
  71.1 441.2 %reduce-scatter.2.cloned.1.call-start = ((), (), s32[]{:S(2)}) async-start(), calls=%async_computation.2 | async-start | bytes 278528 | tf_op jit(solution)/shard_map/reduce_scatter | solution.py:47
  414.2 0.7 copy-start.1
Sparse Core Ops, SparseCore 0:
  71.2 330.5 all-reduce.1
  415.1 97.1 reduce-scatter.1
where the time goes:
time: 520 us; the launch traced here: 519 us
  waiting for transfers between devices  374 us (72%)
  blocking collectives  97 us (19%)
  other arithmetic  23 us (4%)
  between operations  14.8 us (3%)
    psum x1, waiting for transfers between devices, body(): summed = lax.psum(partial_value, 'col')  278 us
    reduce_scatter x1, waiting for transfers between devices, body(): lax.psum_scatter(partial_back, 'row', scatter_dimension=0, tiled=True)  96 us
    all_gather x1, blocking collectives, body(): scales = lax.all_gather(diag_rows, 'col', axis=0, tiled=True)  52.4 us
    all_gather x1, blocking collectives, body(): column_vectors = lax.all_gather(x_cols, 'row', axis=1, tiled=True)  44.6 us
    scatter-add x1, other arithmetic, body(): jax.ops.segment_sum(products, rows_here, num_segments=block_rows)  10.8 us
  transfers between devices with their start and end apart: 2, of which 2 were waited for; matrix products, arithmetic and copies ran while one was open for 0% of the time, Pallas kernels for 0%

commit v1 on v0

--- a/solution.py
+++ b/solution.py
@@ -34,7 +34,10 @@
     shift_term = -theta[None, :, None] * column_tiles.astype(jnp.float32) * on_diag
     current = lax.dynamic_slice_in_dim(partial_value, offset, block_cols, 0)
     partial_value = lax.dynamic_update_slice_in_dim(partial_value, current + shift_term, offset, 0)
-    scales = lax.all_gather(diag_rows, "col", axis=0, tiled=True)
+    x_next = lax.axis_size("col")
+    arr_now = jnp.stack([diag_rows] * x_next)
+    local_now = lax.all_to_all(arr_now, "col", 0, 0)
+    scales = jnp.concatenate(local_now, axis=0)
     summed = lax.psum(partial_value, "col")
     scaled = (summed / scales.reshape(-1, 1, tile_width)).astype(jnp.bfloat16)
     resid_part = lax.dynamic_slice_in_dim(summed, lax.axis_index("col") * share_rows, share_rows, 0)

time: 520 us -> 520 us (level)
  blocking collectives: 97 us -> 44.6 us
  waiting for transfers between devices: 374 us -> 410 us
  starting transfers between devices: 0.08 us -> 15.7 us
    all_gather x1 -> x0, blocking collectives: 52.4 us -> none  [body(): scales = lax.all_gather(diag_rows, 'col', axis=0, tiled=True)]
    psum x1, waiting for transfers between devices: 278 us -> 301 us  [body(): summed = lax.psum(partial_value, 'col')]
    all_to_all x0 -> x1, starting transfers between devices: none -> 15.6 us  [body(): local_now = lax.all_to_all(arr_now, 'col', 0, 0)]
    all_to_all x0 -> x1, waiting for transfers between devices: none -> 13.5 us  [body(): local_now = lax.all_to_all(arr_now, 'col', 0, 0)]
  transfers between devices with their start and end apart: 2 -> 3, of which waited for: 2 -> 3; matrix products, arithmetic and copies ran while one was open for 0% -> 0% of each run, Pallas kernels for 0% -> 0%
where the time goes in v1:
time: 520 us; the launch traced here: 519 us
  waiting for transfers between devices  410 us (79%)
  blocking collectives  44.6 us (9%)
  other arithmetic  22.9 us (4%)
  starting transfers between devices  15.7 us (3%)
  between operations  14.8 us (3%)
  local copies, waits for them, and re-layouts  5.54 us (1%)
    psum x1, waiting for transfers between devices, body(): summed = lax.psum(partial_value, 'col')  301 us
    reduce_scatter x1, waiting for transfers between devices, body(): lax.psum_scatter(partial_back, 'row', scatter_dimension=0, tiled=True)  95.9 us
    all_gather x1, blocking collectives, body(): column_vectors = lax.all_gather(x_cols, 'row', axis=1, tiled=True)  44.6 us
    all_to_all x1, starting transfers between devices, body(): local_now = lax.all_to_all(arr_now, 'col', 0, 0)  15.6 us
    all_to_all x1, waiting for transfers between devices, body(): local_now = lax.all_to_all(arr_now, 'col', 0, 0)  13.5 us
    scatter-add x1, other arithmetic, body(): jax.ops.segment_sum(products, rows_here, num_segments=block_rows)  10.8 us
  transfers between devices with their start and end apart: 3, of which 3 were waited for; matrix products, arithmetic and copies ran while one was open for 0% of the time, Pallas kernels for 0%

profile of v1, /device:TPU:8, one launch (start us, length us, event | category | flops | bytes accessed | tf_op | source)
XLA Modules:
  0.0 519.1 jit_solution(16784262700681945723)
XLA Ops:
  7.2 0.0 copy-start
  7.2 0.0 copy-start.4
  7.2 0.0 all-reduce.2.cloned.1.call-start
  7.2 44.6 %all_gather.3 = bf16[8,8192]{1,0:T(8,128)(2,1)S(1)} all-gather(bf16[8,512]{1,0:T(8,128)(2,1)} %param.7), channel_id=1, replica_groups=mesh['row'=16,'col'=32] {'row'}, dimensions={1}, use_global_device_ids=true | all-gather | bytes 139264 | tf_op jit(solution)/shard_map/all_gather | solution.py:26
  51.8 0.7 fusion.16
  53.1 0.7 compare_and_fusion.1
  53.8 0.7 neg.4
  54.5 0.7 gather_fusion
  55.1 0.0 copy-done
  55.1 0.0 copy-start.3
  55.2 2.5 fusion.4
  57.7 0.8 broadcast_in_dim.43
  58.5 0.0 copy-done.4
  58.5 10.8 %scatter_fusion = f32[128,8,128]{2,1,0:T(8,128)} fusion(f32[128,8,128]{2,1,0:T(8,128)} %broadcast_in_dim.43, s32[96]{0:T(128)S(1)} %bitcast.38, f32[96,8,128]{2,1,0:T(8,128)} %fusion.4), kind=kCustom, calls=%fused_computation.2 | custom fusion | flops 98304 | bytes 1180032 | tf_op jit(solution)/shard_map/scatter-add | solution.py:31
  69.3 1.7 add_dynamic-update-slice_fusion
  71.1 0.0 copy-start.2
  71.1 0.0 all-reduce.2.cloned.1.call-update
  71.1 0.0 copy-done.3
  71.1 0.7 stack.2
  71.8 15.6 %all-to-all-start = ((f32[32,1,512]{2,1,0:T(1,128)}), f32[32,1,512]{2,1,0:T(1,128)S(1)}, u32[]{:S(2)}, u32[]{:S(2)}) async-start(f32[32,1,512]{2,1,0:T(1,128)} %stack.2), calls=%async_computation | async-start | bytes 131072 | tf_op jit(solution)/shard_map/all_to_all | solution.py:39
  87.4 0.0 reduce-scatter.2.cloned.1.call-start
  87.5 13.5 %all-to-all-done = f32[32,1,512]{2,1,0:T(1,128)S(1)} async-done(((f32[32,1,512]{2,1,0:T(1,128)}), f32[32,1,512]{2,1,0:T(1,128)S(1)}, u32[]{:S(2)}, u32[]{:S(2)}) %all-to-all-start) | async-done | bytes 65568 | tf_op jit(solution)/shard_map/all_to_all | solution.py:39
  101.0 300.9 %all-reduce.2.cloned.1.call-done = f32[128,8,128]{2,1,0:T(8,128)} async-done(((f32[128,8,128]{2,1,0:T(8,128)}), f32[128,8,128]{2,1,0:T(8,128)}) %all-reduce.2.cloned.1.call-update) | async-done | bytes 524304 | tf_op jit(solution)/shard_map/psum | solution.py:41
  401.9 1.1 divide_convert_fusion
  403.0 1.3 gather_fusion.1
  404.4 2.6 fusion.7
  407.0 0.0 copy-done.2
  407.0 7.3 %scatter_fusion.1 = f32[64,8,128]{2,1,0:T(8,128)S(1)} fusion(f32[64,8,128]{2,1,0:T(8,128)S(1)} %broadcast_in_dim.48, s32[96]{0:T(128)S(1)} %bitcast.37, f32[96,8,128]{2,1,0:T(8,128)} %fusion.7), kind=kCustom, calls=%fused_computation.3 | custom fusion | flops 98304 | bytes 1180032 | tf_op jit(solution)/shard_map/scatter-add | solution.py:49
  414.3 0.0 copy-start.1
  414.3 0.7 copy-done.1
  415.0 0.0 reduce-scatter.2.cloned.1.call-update
  415.0 1.3 dynamic-slice_bitcast_fusion
  416.4 95.9 %reduce-scatter.2.cloned.1.call-done = f32[4,8,128]{2,1,0:T(8,128)} async-done(((f32[64,8,128]{2,1,0:T(8,128)}), f32[4,8,128]{2,1,0:T(8,128)}) %reduce-scatter.2.cloned.1.call-update) | async-done | bytes 16400 | tf_op jit(solution)/shard_map/reduce_scatter | solution.py:50
  (5 shorter events, 0.0 us)
Async XLA Ops:
  7.2 48.0 %copy-start = (bf16[1,1,96,128,128]{4,3,2,1,0:T(8,128)(2,1)S(1)}, bf16[1,1,96,128,128]{4,3,2,1,0:T(8,128)(2,1)}, u32[]{:S(2)}) copy-start(bf16[1,1,96,128,128]{4,3,2,1,0:T(8,128)(2,1)} %param.10) | copy-start | bytes 9437188
  7.2 51.3 %copy-start.4 = (s32[1,1,96]{2,1,0:T(1,128)S(1)}, s32[1,1,96]{2,1,0:T(1,128)}, u32[]{:S(2)}) copy-start(s32[1,1,96]{2,1,0:T(1,128)} %param.11) | copy-start | bytes 1156
  7.2 394.7 %all-reduce.2.cloned.1.call-start = ((), (), s32[]{:S(2)}) async-start(), calls=%async_computation.2 | async-start | bytes 1048576 | tf_op jit(solution)/shard_map/psum | solution.py:41
  55.1 16.0 %copy-start.3 = (f32[512]{0:T(512)S(1)}, f32[512]{0:T(512)}, u32[]{:S(2)}) copy-start(f32[512]{0:T(512)} %param.8) | copy-start | bytes 6148
  71.1 335.9 %copy-start.2 = (s32[1,1,96]{2,1,0:T(1,128)S(1)}, s32[1,1,96]{2,1,0:T(1,128)}, u32[]{:S(2)}) copy-start(s32[1,1,96]{2,1,0:T(1,128)} %param.12) | copy-start | bytes 1156
  71.8 29.2 %all-to-all-start = ((f32[32,1,512]{2,1,0:T(1,128)}), f32[32,1,512]{2,1,0:T(1,128)S(1)}, u32[]{:S(2)}, u32[]{:S(2)}) async-start(f32[32,1,512]{2,1,0:T(1,128)} %stack.2), calls=%async_computation | async-start | bytes 131072 | tf_op jit(solution)/shard_map/all_to_all | solution.py:39
  87.4 424.9 %reduce-scatter.2.cloned.1.call-start = ((), (), s32[]{:S(2)}) async-start(), calls=%async_computation.3 | async-start | bytes 278528 | tf_op jit(solution)/shard_map/reduce_scatter | solution.py:50
  414.3 0.7 copy-start.1
Sparse Core Ops, SparseCore 0:
  71.2 330.6 all-reduce.1
  415.1 97.1 reduce-scatter.1

commit v2 on v0

--- a/solution.py
+++ b/solution.py
@@ -35,7 +35,8 @@
     current = lax.dynamic_slice_in_dim(partial_value, offset, block_cols, 0)
     partial_value = lax.dynamic_update_slice_in_dim(partial_value, current + shift_term, offset, 0)
     scales = lax.all_gather(diag_rows, "col", axis=0, tiled=True)
-    summed = lax.psum(partial_value, "col")
+    parts = lax.all_gather(partial_value, "col", axis=0, tiled=False)
+    summed = parts.sum(axis=0)
     scaled = (summed / scales.reshape(-1, 1, tile_width)).astype(jnp.bfloat16)
     resid_part = lax.dynamic_slice_in_dim(summed, lax.axis_index("col") * share_rows, share_rows, 0)
     picked_rows = jnp.take(scaled, rows_here, axis=0)

time: 520 us -> 404 us (0.78)
  waiting for transfers between devices: 374 us -> 243 us
  other arithmetic: 23 us -> 29.7 us
  blocking collectives: 97 us -> 103 us
    psum x1 -> x0, waiting for transfers between devices: 278 us -> none  [body(): summed = lax.psum(partial_value, 'col')]
    all_gather x0 -> x1, waiting for transfers between devices: none -> 160 us  [body(): parts = lax.all_gather(partial_value, 'col', axis=0, tiled=False)]
    reduce_scatter x1, waiting for transfers between devices: 96 us -> 82.9 us  [body(): lax.psum_scatter(partial_back, 'row', scatter_dimension=0, tiled=True)]
    reduce_sum x0 -> x1, other arithmetic: none -> 7.35 us  [body(): summed = parts.sum(axis=0)]
    all_gather x1, blocking collectives: 52.4 us -> 58.7 us  [body(): scales = lax.all_gather(diag_rows, 'col', axis=0, tiled=True)]
where the time goes in v2:
time: 404 us; the launch traced here: 403 us
  waiting for transfers between devices  243 us (60%)
  blocking collectives  103 us (25%)
  other arithmetic  29.7 us (7%)
  between operations  15 us (4%)
  local copies, waits for them, and re-layouts  6.72 us (2%)
  matrix products  5.17 us (1%)
    all_gather x1, waiting for transfers between devices, body(): parts = lax.all_gather(partial_value, 'col', axis=0, tiled=False)  160 us
    reduce_scatter x1, waiting for transfers between devices, body(): lax.psum_scatter(partial_back, 'row', scatter_dimension=0, tiled=True)  82.9 us
    all_gather x1, blocking collectives, body(): scales = lax.all_gather(diag_rows, 'col', axis=0, tiled=True)  58.7 us
    all_gather x1, blocking collectives, body(): column_vectors = lax.all_gather(x_cols, 'row', axis=1, tiled=True)  44.4 us
    scatter-add x1, other arithmetic, body(): jax.ops.segment_sum(products, rows_here, num_segments=block_rows)  10.8 us
  transfers between devices with their start and end apart: 2, of which 2 were waited for; matrix products, arithmetic and copies ran while one was open for 0% of the time, Pallas kernels for 0%

profile of v2, /device:TPU:8, one launch (start us, length us, event | category | flops | bytes accessed | tf_op | source)
XLA Modules:
  0.0 402.7 jit_solution(8119994197836884782)
XLA Ops:
  7.2 0.0 copy-start
  7.2 0.0 copy-start.4
  7.2 0.0 all-gather.3.cloned.1.call-start
  8.1 0.7 fusion.16
  8.8 0.7 compare_and_fusion.1
  9.5 44.4 %all_gather.14 = bf16[8,8192]{1,0:T(8,128)(2,1)S(1)} all-gather(bf16[8,512]{1,0:T(8,128)(2,1)} %param.7), channel_id=1, replica_groups=mesh['row'=16,'col'=32] {'row'}, dimensions={1}, use_global_device_ids=true | all-gather | bytes 139264 | tf_op jit(solution)/shard_map/all_gather | solution.py:26
  53.9 0.7 gather_fusion
  54.6 0.0 copy-done
  54.6 0.0 copy-start.5
  54.6 0.0 copy-start.3
  54.6 2.5 fusion.4
  57.1 0.8 broadcast_in_dim.43
  57.9 0.0 copy-done.4
  57.9 10.8 %scatter_fusion = f32[128,8,128]{2,1,0:T(8,128)} fusion(f32[128,8,128]{2,1,0:T(8,128)} %broadcast_in_dim.43, s32[96]{0:T(128)S(1)} %bitcast.44, f32[96,8,128]{2,1,0:T(8,128)} %fusion.4), kind=kCustom, calls=%fused_computation.2 | custom fusion | flops 98304 | bytes 1180032 | tf_op jit(solution)/shard_map/scatter-add | solution.py:31
  68.7 1.9 copy.10
  70.6 0.0 copy-done.5
  70.6 1.8 bitcast_dynamic-update-slice_fusion
  72.4 0.0 all-gather.3.cloned.1.call-update
  72.4 0.0 reduce-scatter.2.cloned.1.call-start
  72.4 0.0 copy-done.3
  72.4 58.7 %all-gather = f32[32,1,512]{2,1,0:T(1,128)S(1)} all-gather(f32[1,1,512]{2,1,0:T(1,128)S(1)} %bitcast.43), channel_id=1, replica_groups=mesh['row'=16,'col'=32] {'col'}, dimensions={0}, use_global_device_ids=true | all-gather | bytes 67584 | tf_op jit(solution)/shard_map/all_gather | solution.py:37
  131.1 160.0 %all-gather.3.cloned.1.call-done = f32[32,128,8,128]{3,2,1,0:T(8,128)} async-done(((f32[1,128,8,128]{3,2,1,0:T(8,128)}), f32[32,128,8,128]{3,2,1,0:T(8,128)}) %all-gather.3.cloned.1.call-update) | async-done | bytes 16777232 | tf_op jit(solution)/shard_map/all_gather | solution.py:38
  291.2 7.3 %reduce_sum.9 = f32[128,8,128]{2,1,0:T(8,128)} reduce(f32[32,128,8,128]{3,2,1,0:T(8,128)} %all-gather.3.cloned.1.call-done, f32[]{:T(128)} %constant.58.clone.1), dimensions={0}, to_apply=%region_1.2 | reduce | flops 4063232 | bytes 17301508 | tf_op jit(solution)/shard_map/reduce_sum | solution.py:39
  298.5 0.0 copy-start.2
  298.5 1.1 divide_convert_fusion
  299.7 1.3 gather_fusion.1
  301.0 2.7 fusion.7
  303.7 0.0 copy-done.2
  303.7 7.3 %scatter_fusion.1 = f32[64,8,128]{2,1,0:T(8,128)S(1)} fusion(f32[64,8,128]{2,1,0:T(8,128)S(1)} %broadcast_in_dim.48, s32[96]{0:T(128)S(1)} %bitcast.42, f32[96,8,128]{2,1,0:T(8,128)} %fusion.7), kind=kCustom, calls=%fused_computation.3 | custom fusion | flops 98304 | bytes 1180032 | tf_op jit(solution)/shard_map/scatter-add | solution.py:47
  310.9 0.0 copy-start.1
  310.9 0.7 copy-done.1
  311.6 0.0 reduce-scatter.2.cloned.1.call-update
  311.7 1.3 dynamic-slice_bitcast_fusion
  313.0 82.9 %reduce-scatter.2.cloned.1.call-done = f32[4,8,128]{2,1,0:T(8,128)} async-done(((f32[64,8,128]{2,1,0:T(8,128)}), f32[4,8,128]{2,1,0:T(8,128)}) %reduce-scatter.2.cloned.1.call-update) | async-done | bytes 16400 | tf_op jit(solution)/shard_map/reduce_scatter | solution.py:48
  (6 shorter events, 0.0 us)
Async XLA Ops:
  7.2 47.4 %copy-start = (bf16[1,1,96,128,128]{4,3,2,1,0:T(8,128)(2,1)S(1)}, bf16[1,1,96,128,128]{4,3,2,1,0:T(8,128)(2,1)}, u32[]{:S(2)}) copy-start(bf16[1,1,96,128,128]{4,3,2,1,0:T(8,128)(2,1)} %param.10) | copy-start | bytes 9437188
  7.2 50.8 %copy-start.4 = (s32[1,1,96]{2,1,0:T(1,128)S(1)}, s32[1,1,96]{2,1,0:T(1,128)}, u32[]{:S(2)}) copy-start(s32[1,1,96]{2,1,0:T(1,128)} %param.11) | copy-start | bytes 1156
  7.2 284.0 %all-gather.3.cloned.1.call-start = ((), (), s32[]{:S(2)}) async-start(), calls=%async_computation.1 | async-start | bytes 17301504 | tf_op jit(solution)/shard_map/all_gather | solution.py:38
  54.6 16.0 %copy-start.5 = (f32[8]{0:T(128)S(1)}, f32[8]{0:T(128)}, u32[]{:S(2)}) copy-start(f32[8]{0:T(128)} %param.9) | copy-start | bytes 100
  54.6 17.8 %copy-start.3 = (f32[512]{0:T(512)S(1)}, f32[512]{0:T(512)}, u32[]{:S(2)}) copy-start(f32[512]{0:T(512)} %param.8) | copy-start | bytes 6148
  72.4 323.5 %reduce-scatter.2.cloned.1.call-start = ((), (), s32[]{:S(2)}) async-start(), calls=%async_computation.2 | async-start | bytes 278528 | tf_op jit(solution)/shard_map/reduce_scatter | solution.py:48
  298.5 5.1 %copy-start.2 = (s32[1,1,96]{2,1,0:T(1,128)S(1)}, s32[1,1,96]{2,1,0:T(1,128)}, u32[]{:S(2)}) copy-start(s32[1,1,96]{2,1,0:T(1,128)} %param.12) | copy-start | bytes 1156
  310.9 0.7 copy-start.1
Sparse Core Ops, SparseCore 0:
  72.5 218.6 all-gather.2
  311.8 84.0 reduce-scatter.1
